TPU v7x, 32 devices: a whole 2x2x4 slice. The times are simulated.
32 devices in a mesh: wide: 8 (over z, y), narrow: 4 (over x, core).
Axes of the slice: x: 2, y: 2, z: 4, core: 2. Of those that a mesh axis runs over, the one named last changes fastest.
Arguments:
- tau: float32 [512, 40000], P(None, 'narrow'), may hold values from -6 to 6
- vv_integrals: float32 [40000, 1024], P('narrow', 'wide'), may hold values from -0.03125 to 0.03125
- cycle_amps: float32 [512, 12000], P('wide', 'narrow'), may hold values from -6 to 6
- ov_integrals: float32 [12000, 1024], P('narrow', 'wide'), may hold values from -0.0546875 to 0.0546875
Outputs:
- ladder_residual: float32 [512, 1024], P('narrow', 'wide')
- cycle_residual: float32 [512, 1024], P('narrow', 'wide')
All inputs are finite; a program needn't handle non-finite values.
Results may differ from a plain program's by a relative error of at most 0.000071.
Values sent between devices are 32-bit elements; how exact they have to be, the bound alone decides.
A program may use at most 64 MiB of HBM per device.

v0:
```python
import jax
import jax.numpy as jnp
from jax import lax
from jax.sharding import PartitionSpec as P


def contract(left, right):
    return jnp.dot(left, right, precision=lax.Precision.HIGHEST, preferred_element_type=jnp.float32)


def cycle_terms_of(cycle_amps, ov_integrals):
    return contract(lax.all_gather(cycle_amps, "wide", axis=0, tiled=True), ov_integrals)


def body(tau, vv_integrals, cycle_amps, ov_integrals):
    ladder_terms = contract(tau, vv_integrals)
    ladder_residual = lax.psum_scatter(ladder_terms, "narrow", scatter_dimension=0, tiled=True)
    cycle_terms = cycle_terms_of(cycle_amps, ov_integrals)
    cycle_residual = lax.psum_scatter(cycle_terms, "narrow", scatter_dimension=0, tiled=True)
    return (ladder_residual, cycle_residual)


def solution(mesh):
    in_specs = (P(None, "narrow"), P("narrow", "wide"), P("wide", "narrow"), P("narrow", "wide"))
    out_specs = (P("narrow", "wide"), P("narrow", "wide"))
    return jax.shard_map(body, mesh=mesh, in_specs=in_specs, out_specs=out_specs, check_vma=False)
```

profile of v0, /device:TPU:0, one launch (start us, length us, event | category | flops | bytes accessed | tf_op | source)
XLA Modules:
  0.0 146.6 jit_solution(4315122933022071871)
XLA Ops:
  8.0 0.0 copy-start
  8.0 0.0 all-gather.2.cloned.1.call-start
  8.1 0.7 all-gather.2.cloned.1.call-update
  8.7 0.0 reduce-scatter.3.cloned.1.call-start
  8.8 36.7 %fusion = f32[512,128]{1,0:T(8,128)} fusion(f32[512,10000]{0,1:T(8,128)} %param.4, f32[10000,128]{1,0:T(8,128)} %param.5), kind=kOutput, calls=%fused_computation | convolution fusion | flops 7864320000 | bytes 25862144 | tf_op jit(solution)/shard_map/dot_general | solution.py:8
  45.5 0.0 reduce-scatter.3.cloned.1.call-update
  45.5 0.0 reduce-scatter.5.cloned.1.call-start
  45.6 67.4 %all-gather.2.cloned.1.call-done = f32[512,3000]{1,0:T(8,128)} async-done(((f32[64,3000]{1,0:T(8,128)}), f32[512,3000]{1,0:T(8,128)}) %all-gather.2.cloned.1.call-update) | async-done | bytes 6144016 | tf_op jit(solution)/shard_map/all_gather | solution.py:12
  113.0 0.0 copy-done
  113.0 7.8 %fusion.1 = f32[512,128]{1,0:T(8,128)} fusion(f32[512,3000]{1,0:T(8,128)} %all-gather.2.cloned.1.call-done, f32[3000,128]{1,0:T(8,128)S(1)} %copy-done), kind=kOutput, calls=%fused_computation.1 | convolution fusion | flops 2359296000 | bytes 7942144 | tf_op jit(solution)/shard_map/dot_general | solution.py:8
  120.9 0.0 reduce-scatter.5.cloned.1.call-update
  120.9 0.0 reduce-scatter.3.cloned.1.call-done
  120.9 18.2 %reduce-scatter.5.cloned.1.call-done = f32[128,128]{1,0:T(8,128)} async-done(((f32[512,128]{1,0:T(8,128)}), f32[128,128]{1,0:T(8,128)}) %reduce-scatter.5.cloned.1.call-update) | async-done | bytes 65552 | tf_op jit(solution)/shard_map/reduce_scatter | solution.py:19
Async XLA Ops:
  8.0 105.0 %copy-start = (f32[3000,128]{1,0:T(8,128)S(1)}, f32[3000,128]{1,0:T(8,128)}, u32[]{:S(2)}) copy-start(f32[3000,128]{1,0:T(8,128)} %param.7) | copy-start | bytes 4608004
  8.0 105.0 %all-gather.2.cloned.1.call-start = ((), (), s32[]{:S(2)}) async-start(), calls=%async_computation.3 | async-start | bytes 7077888 | tf_op jit(solution)/shard_map/all_gather | solution.py:12
  8.7 112.2 %reduce-scatter.3.cloned.1.call-start = ((), (), s32[]{:S(2)}) async-start(), calls=%async_computation.2 | async-start | bytes 327680 | tf_op jit(solution)/shard_map/reduce_scatter | solution.py:17
  45.5 93.6 %reduce-scatter.5.cloned.1.call-start = ((), (), s32[]{:S(2)}) async-start(), calls=%async_computation.4 | async-start | bytes 327680 | tf_op jit(solution)/shard_map/reduce_scatter | solution.py:19
Sparse Core Ops, SparseCore 0:
  11.3 101.7 all-gather.1
Sparse Core Ops, SparseCore 1:
  45.6 22.7 reduce-scatter.2
  121.0 18.1 reduce-scatter.4
where the time goes:
time: 147 us
  waiting for transfers between devices  86.4 us (59%)
  matrix products  44.6 us (30%)
  between operations  15.5 us (11%)
    all_gather x1, waiting for transfers between devices, cycle_terms_of(): lax.all_gather(cycle_amps, 'wide', axis=0, tiled=True)  67.4 us
    dot_general x2, matrix products, contract(): jnp.dot(left, right, precision=lax.Precision.HIGHEST, preferred_element_t...  44.6 us
    reduce_scatter x1, waiting for transfers between devices, body(): lax.psum_scatter(cycle_terms, 'narrow', scatter_dimension=0, tiled=True)  18.2 us
  transfers between devices with their start and end apart: 3, of which 2 were waited for; matrix products, arithmetic and copies ran while one was open for 30% of the time, Pallas kernels for 0%

commit v1 on v0

v1 whole, which is shorter than its diff:
```python
import functools

import jax
import jax.numpy as jnp
from jax import lax
from jax.experimental import pallas as pl
from jax.experimental.pallas import tpu as pltpu
from jax.sharding import PartitionSpec as P

MESH = pl.DeviceIdType.MESH
F32 = jnp.float32
BF16 = jnp.bfloat16
STEP_Y = 4


def halves(x):
    hi = x.astype(BF16)
    lo = (x - hi.astype(F32)).astype(BF16)
    return hi, lo


def dot(a, b):
    return jnp.dot(a, b, preferred_element_type=F32)


def kernel(depth, tk, steps, kh,
           tau_ref, vv_ref, amps_ref, ov_ref, lad_ref, cyc_ref,
           a_buf, a_send, b_buf, b_send, b_hi, b_lo, acc, part, rs_c, rs_l,
           zr_send, zl_send, a_recv, y_send, b_recv, c_send, c_recv, l_send, l_recv):
    s = pl.program_id(0)
    w, n = lax.axis_index("wide"), lax.axis_index("narrow")
    z = w // 2
    y = w - 2 * z
    yp = 2 * z + 1 - y
    cols = ov_ref.shape[1]
    rows = amps_ref.shape[0]
    own = amps_ref.shape[1]
    rest = own - kh

    def a_copy(zs, j, dz):
        send = zr_send if dz > 0 else zl_send
        return pltpu.make_async_remote_copy(
            src_ref=a_buf.at[zs, j], dst_ref=a_buf.at[zs, j], send_sem=send.at[zs, j],
            recv_sem=a_recv.at[zs, j], device_id=(w + 2 * dz, n), device_id_type=MESH)

    def ya_copy():
        return pltpu.make_async_remote_copy(
            src_ref=a_send, dst_ref=a_buf.at[z, 1], send_sem=y_send.at[0],
            recv_sem=a_recv.at[z, 1], device_id=(yp, n), device_id_type=MESH)

    def yb_copy():
        return pltpu.make_async_remote_copy(
            src_ref=b_send, dst_ref=b_buf.at[1], send_sem=y_send.at[1],
            recv_sem=b_recv, device_id=(yp, n), device_id_type=MESH)

    def c_copy(zs, j, slot):
        return pltpu.make_async_remote_copy(
            src_ref=part.at[zs, j], dst_ref=rs_c.at[slot, j], send_sem=c_send.at[zs, j],
            recv_sem=c_recv.at[slot, j], device_id=(w if j == 0 else yp, zs), device_id_type=MESH)

    def l_copy(zs, slot):
        return pltpu.make_async_remote_copy(
            src_ref=acc.at[pl.ds(zs * 128, 128)], dst_ref=rs_l.at[slot], send_sem=l_send.at[zs],
            recv_sem=l_recv.at[slot], device_id=(w, zs), device_id_type=MESH)

    @pl.when(s == 0)
    def _():
        barrier = pltpu.get_barrier_semaphore()
        for k in range(4):
            @pl.when(n != k)
            def _():
                pl.semaphore_signal(barrier, inc=1, device_id=(w, k), device_id_type=MESH)
            pl.semaphore_signal(barrier, inc=1, device_id=(yp, k), device_id_type=MESH)

        @pl.when(z > 0)
        def _():
            pl.semaphore_signal(barrier, inc=1, device_id=(w - 2, n), device_id_type=MESH)

        @pl.when(z < 3)
        def _():
            pl.semaphore_signal(barrier, inc=1, device_id=(w + 2, n), device_id_type=MESH)

        tail = kh - 128

        @pl.when(y == 0)
        def _():
            a_buf[z, 0] = amps_ref[:, :kh]
            a_send[:, tail:] = jnp.zeros((rows, 128), F32)
            a_send[:, :rest] = amps_ref[:, kh:own]

        @pl.when(y == 1)
        def _():
            a_buf[z, 0, :, tail:] = jnp.zeros((rows, 128), F32)
            a_buf[z, 0, :, :rest] = amps_ref[:, kh:own]
            a_send[...] = amps_ref[:, :kh]

        @pl.when((z == 0) | (z == 3))
        def _():
            pl.semaphore_wait(barrier, 8)

        @pl.when((z == 1) | (z == 2))
        def _():
            pl.semaphore_wait(barrier, 9)

        ya_copy().start()

        @pl.when(z < 3)
        def _():
            a_copy(z, 0, 1).start()

        @pl.when(z > 0)
        def _():
            a_copy(z, 0, -1).start()

        @pl.when(y == 0)
        def _():
            b_buf[0] = ov_ref[:kh]
            b_send[:rest] = ov_ref[kh:own]
            b_send[rest:] = jnp.zeros((kh - rest, cols), F32)

        @pl.when(y == 1)
        def _():
            b_buf[0, :rest] = ov_ref[kh:own]
            b_buf[0, rest:] = jnp.zeros((kh - rest, cols), F32)
            b_send[...] = ov_ref[:kh]

        acc[...] = jnp.zeros(acc.shape, F32)

    @pl.when(s == STEP_Y)
    def _():
        ya_copy().wait_recv()

        @pl.when(z < 3)
        def _():
            a_copy(z, 1, 1).start()

        @pl.when(z > 0)
        def _():
            a_copy(z, 1, -1).start()

        yb_copy().start()

    def ladder(a, b):
        ah, al = halves(a)
        bh, bl = halves(b)
        both = dot(ah, jnp.concatenate([bh, bl], axis=1))
        acc[...] += both[:, :cols] + both[:, cols:] + dot(al, bh)

    @pl.when(s < steps - 1)
    def _():
        ladder(tau_ref[...], vv_ref[...])

    def row_block(zs):
        ah, al = halves(a_buf[zs].reshape(2 * rows, kh))
        r = dot(ah, b_hi[...]) + dot(ah, b_lo[...]) + dot(al, b_hi[...])
        mine = pl.ds(pl.multiple_of(y * rows, rows), rows)
        other = pl.ds(pl.multiple_of((1 - y) * rows, rows), rows)
        for j in range(2):
            part[zs, j, mine, :] = r[:rows, j * cols:(j + 1) * cols]
            part[zs, j, other, :] = r[rows:, j * cols:(j + 1) * cols]

        @pl.when(zs != n)
        def _():
            c_copy(zs, 0, n).start()
        c_copy(zs, 1, n).start()

    def arrive(d, j):
        @pl.when(z >= d)
        def _():
            a_copy(z - d, j, 1).wait_recv()
            if d < 3:
                @pl.when(z < 3)
                def _():
                    a_copy(z - d, j, 1).start()

        @pl.when(z + d <= 3)
        def _():
            a_copy(z + d, j, -1).wait_recv()
            if d < 3:
                @pl.when(z > 0)
                def _():
                    a_copy(z + d, j, -1).start()

    def left_block(d):
        @pl.when(z >= d)
        def _():
            row_block(z - d)

    def right_block(d):
        @pl.when(z + d <= 3)
        def _():
            row_block(z + d)

    @pl.when(s == steps - 1)
    def _():
        last = depth - (steps - 1) * tk
        a = tau_ref[...]
        a = jnp.where(lax.broadcasted_iota(jnp.int32, a.shape, 1) < last, a, 0.0)
        b = vv_ref[...]
        b = jnp.where(lax.broadcasted_iota(jnp.int32, b.shape, 0) < last, b, 0.0)
        ladder(a, b)
        arrive(1, 0)
        for k in range(4):
            @pl.when(n != k)
            def _():
                l_copy(k, n).start()
        arrive(1, 1)
        yb_copy().wait_recv()
        for j in range(2):
            hi, lo = halves(b_buf[j])
            b_hi[:, j * cols:(j + 1) * cols] = hi
            b_lo[:, j * cols:(j + 1) * cols] = lo
        row_block(z)
        arrive(2, 0)
        left_block(1)
        right_block(1)
        arrive(2, 1)
        left_block(2)
        right_block(2)
        total = acc[pl.ds(pl.multiple_of(n * 128, 128), 128), :]
        for k in range(4):
            @pl.when(n != k)
            def _():
                l_copy(k, k).wait_recv()
                l_copy(k, n).wait_send()

            @pl.when(n == k)
            def _():
                rs_l[k] = jnp.zeros((128, cols), F32)
            total += rs_l[k]
        lad_ref[...] = total
        arrive(3, 0)
        arrive(3, 1)
        left_block(3)
        right_block(3)
        total = part[n, 0]
        for k in range(4):
            @pl.when(n != k)
            def _():
                c_copy(k, 0, k).wait_recv()
                c_copy(k, 0, n).wait_send()

            @pl.when(n == k)
            def _():
                rs_c[k, 0] = jnp.zeros((128, cols), F32)
            c_copy(k, 1, k).wait_recv()
            c_copy(k, 1, n).wait_send()
            total += rs_c[k, 0] + rs_c[k, 1]
        cyc_ref[...] = total
        ya_copy().wait_send()
        yb_copy().wait_send()
        for j in range(2):
            for k in range(4):
                @pl.when((z < 3) & (z >= k))
                def _():
                    a_copy(k, j, 1).wait_send()

                @pl.when((z > 0) & (z <= k))
                def _():
                    a_copy(k, j, -1).wait_send()


def fused(tau, vv_integrals, cycle_amps, ov_integrals):
    depth = tau.shape[1]
    cols = vv_integrals.shape[1]
    rows, own = cycle_amps.shape
    kh = -(-own // 256) * 128
    tk = 1280
    steps = -(-depth // tk)
    sem = pltpu.SemaphoreType.DMA
    out = jax.ShapeDtypeStruct((128, cols), F32)
    return pl.pallas_call(
        functools.partial(kernel, depth, tk, steps, kh),
        grid=(steps,),
        out_shape=(out, out),
        in_specs=[
            pl.BlockSpec((tau.shape[0], tk), lambda s: (0, s)),
            pl.BlockSpec((tk, cols), lambda s: (s, 0)),
            pl.BlockSpec((rows, own), lambda s: (0, 0)),
            pl.BlockSpec((own, cols), lambda s: (0, 0)),
        ],
        out_specs=(pl.BlockSpec((128, cols), lambda s: (0, 0)), pl.BlockSpec((128, cols), lambda s: (0, 0))),
        scratch_shapes=[
            pltpu.VMEM((4, 2, rows, kh), F32),
            pltpu.VMEM((rows, kh), F32),
            pltpu.VMEM((2, kh, cols), F32),
            pltpu.VMEM((kh, cols), F32),
            pltpu.VMEM((kh, 2 * cols), BF16),
            pltpu.VMEM((kh, 2 * cols), BF16),
            pltpu.VMEM((512, cols), F32),
            pltpu.VMEM((4, 2, 128, cols), F32),
            pltpu.VMEM((4, 2, 128, cols), F32),
            pltpu.VMEM((4, 128, cols), F32),
            sem((4, 2)), sem((4, 2)), sem((4, 2)), sem((2,)), sem,
            sem((4, 2)), sem((4, 2)), sem((4,)), sem((4,)),
        ],
        compiler_params=pltpu.CompilerParams(
            collective_id=0, has_side_effects=True, vmem_limit_bytes=56 * 1024 * 1024,
            dimension_semantics=("arbitrary",)),
        cost_estimate=pl.CostEstimate(flops=6 * 512 * depth * cols, bytes_accessed=4 * 512 * depth, transcendentals=0),
    )(tau, vv_integrals, cycle_amps, ov_integrals)


def contract(left, right):
    return jnp.dot(left, right, precision=lax.Precision.HIGHEST, preferred_element_type=F32)


def plain(tau, vv_integrals, cycle_amps, ov_integrals):
    ladder_terms = contract(tau, vv_integrals)
    ladder_residual = lax.psum_scatter(ladder_terms, "narrow", scatter_dimension=0, tiled=True)
    cycle_terms = contract(lax.all_gather(cycle_amps, "wide", axis=0, tiled=True), ov_integrals)
    cycle_residual = lax.psum_scatter(cycle_terms, "narrow", scatter_dimension=0, tiled=True)
    return (ladder_residual, cycle_residual)


def solution(mesh):
    in_specs = (P(None, "narrow"), P("narrow", "wide"), P("wide", "narrow"), P("narrow", "wide"))
    out_specs = (P("narrow", "wide"), P("narrow", "wide"))
    small = mesh.shape["wide"] == 8 and mesh.shape["narrow"] == 4
    return jax.shard_map(fused if small else plain, mesh=mesh, in_specs=in_specs, out_specs=out_specs, check_vma=False)
```

time: 147 us -> 89 us (0.61)
  waiting for transfers between devices: 86.4 us -> 0 us
  Pallas kernels: 0 us -> 64.7 us
  matrix products: 44.6 us -> 0 us
  local copies, waits for them, and re-layouts: 0.01 us -> 22.6 us
  between operations: 15.5 us -> 0.64 us
    all_gather x1 -> x0, waiting for transfers between devices: 67.4 us -> none  [cycle_terms_of(): lax.all_gather(cycle_amps, 'wide', axis=0, tiled=True)]
    pallas_call x0 -> x1, Pallas kernels: none -> 64.7 us  [fused(): pl.pallas_call(functools.partial(kernel, depth, tk, steps, kh), grid=(ste...]
    dot_general x2 -> x0, matrix products: 44.6 us -> none  [contract(): jnp.dot(left, right, precision=lax.Precision.HIGHEST, preferred_element_t...]
    unnamed x2 -> x3, local copies, waits for them, and re-layouts: 0.01 us -> 22.6 us
    reduce_scatter x2 -> x0, waiting for transfers between devices: 18.2 us -> none  [the longest x1 18.2 us: body(): lax.psum_scatter(cycle_terms, 'narrow', scatter_dimension=0, tiled=True)]
  transfers between devices with their start and end apart: 3 -> 0, of which waited for: 2 -> 0; matrix products, arithmetic and copies ran while one was open for 30% -> 0% of each run, Pallas kernels for 0% -> 0%
where the time goes in v1:
time: 89 us; the launch traced here: 88 us
  Pallas kernels  64.7 us (73%)
  local copies, waits for them, and re-layouts  22.6 us (25%)
    pallas_call x1, Pallas kernels, fused(): pl.pallas_call(functools.partial(kernel, depth, tk, steps, kh), grid=(ste...  64.7 us
    unnamed x3, local copies, waits for them, and re-layouts  22.6 us

profile of v1, /device:TPU:0, one launch (start us, length us, event | category | flops | bytes accessed | tf_op | source)
XLA Modules:
  0.0 88.0 jit_solution(919075215310199590)
XLA Ops:
  0.6 19.7 %copy.6.tau_ref = f32[512,10000]{1,0:T(8,128)} copy(f32[512,10000]{0,1:T(8,128)} %param.4) | data formatting | bytes 40960000 | tf_op args[0]
  20.3 64.7 %shard_map.59 = (f32[128,128]{1,0:T(8,128)}, f32[128,128]{1,0:T(8,128)}) custom-call(f32[512,10000]{1,0:T(8,128)} %copy.6.tau_ref, f32[10000,128]{1,0:T(8,128)} %vv_ref.1, f32[64,3000]{1,0:T(8,128)} %amps_ref.1, f32[3000,128]{1,0:T(8,128)} %ov_ref.1), custom_call_target="tpu_custom_call" | custom-call | flops 3932160000 | bytes 20480000 | tf_op jit(solution)/shard_map/pallas_call | solution.py:272
  85.0 1.5 %copy.9 = f32[128,128]{1,0:T(8,128)} copy(f32[128,128]{1,0:T(8,128)} %get-tuple-element.4) | data formatting | bytes 131072
  86.5 1.5 %copy.10 = f32[128,128]{1,0:T(8,128)} copy(f32[128,128]{1,0:T(8,128)} %get-tuple-element.5) | data formatting | bytes 131072

commit v2 on v1

--- a/solution.py
+++ b/solution.py
@@ -24,8 +24,8 @@
 
 
 def kernel(depth, tk, steps, kh,
-           tau_ref, vv_ref, amps_ref, ov_ref, lad_ref, cyc_ref,
-           a_buf, a_send, b_buf, b_send, b_hi, b_lo, acc, part, rs_c, rs_l,
+           tau_ref, vv_ref, amps_ref, ov_ref, out_ref,
+           a_buf, a_send, b_buf, b_send, b_hi, b_lo, acc_t, acc, part, rs_c, rs_l,
            zr_send, zl_send, a_recv, y_send, b_recv, c_send, c_recv, l_send, l_recv):
     s = pl.program_id(0)
     w, n = lax.axis_index("wide"), lax.axis_index("narrow")
@@ -124,7 +124,7 @@
             b_buf[0, rest:] = jnp.zeros((kh - rest, cols), F32)
             b_send[...] = ov_ref[:kh]
 
-        acc[...] = jnp.zeros(acc.shape, F32)
+        acc_t[...] = jnp.zeros(acc_t.shape, F32)
 
     @pl.when(s == STEP_Y)
     def _():
@@ -142,9 +142,9 @@
 
     def ladder(a, b):
         ah, al = halves(a)
-        bh, bl = halves(b)
-        both = dot(ah, jnp.concatenate([bh, bl], axis=1))
-        acc[...] += both[:, :cols] + both[:, cols:] + dot(al, bh)
+        bh, bl = halves(b.T)
+        both = dot(jnp.concatenate([bh, bl], axis=0), ah)
+        acc_t[...] += both[:cols] + both[cols:] + dot(bh, al)
 
     @pl.when(s < steps - 1)
     def _():
@@ -195,10 +195,11 @@
     def _():
         last = depth - (steps - 1) * tk
         a = tau_ref[...]
-        a = jnp.where(lax.broadcasted_iota(jnp.int32, a.shape, 1) < last, a, 0.0)
+        a = jnp.where(lax.broadcasted_iota(jnp.int32, a.shape, 0) < last, a, 0.0)
         b = vv_ref[...]
         b = jnp.where(lax.broadcasted_iota(jnp.int32, b.shape, 0) < last, b, 0.0)
         ladder(a, b)
+        acc[...] = acc_t[...].T
         arrive(1, 0)
         for k in range(4):
             @pl.when(n != k)
@@ -228,7 +229,7 @@
             def _():
                 rs_l[k] = jnp.zeros((128, cols), F32)
             total += rs_l[k]
-        lad_ref[...] = total
+        out_ref[0] = total
         arrive(3, 0)
         arrive(3, 1)
         left_block(3)
@@ -246,7 +247,7 @@
             c_copy(k, 1, k).wait_recv()
             c_copy(k, 1, n).wait_send()
             total += rs_c[k, 0] + rs_c[k, 1]
-        cyc_ref[...] = total
+        out_ref[1] = total
         ya_copy().wait_send()
         yb_copy().wait_send()
         for j in range(2):
@@ -268,18 +269,17 @@
     tk = 1280
     steps = -(-depth // tk)
     sem = pltpu.SemaphoreType.DMA
-    out = jax.ShapeDtypeStruct((128, cols), F32)
-    return pl.pallas_call(
+    both = pl.pallas_call(
         functools.partial(kernel, depth, tk, steps, kh),
         grid=(steps,),
-        out_shape=(out, out),
+        out_shape=jax.ShapeDtypeStruct((2, 128, cols), F32),
         in_specs=[
-            pl.BlockSpec((tau.shape[0], tk), lambda s: (0, s)),
+            pl.BlockSpec((tk, tau.shape[0]), lambda s: (s, 0)),
             pl.BlockSpec((tk, cols), lambda s: (s, 0)),
             pl.BlockSpec((rows, own), lambda s: (0, 0)),
             pl.BlockSpec((own, cols), lambda s: (0, 0)),
         ],
-        out_specs=(pl.BlockSpec((128, cols), lambda s: (0, 0)), pl.BlockSpec((128, cols), lambda s: (0, 0))),
+        out_specs=pl.BlockSpec((2, 128, cols), lambda s: (0, 0, 0)),
         scratch_shapes=[
             pltpu.VMEM((4, 2, rows, kh), F32),
             pltpu.VMEM((rows, kh), F32),
@@ -287,6 +287,7 @@
             pltpu.VMEM((kh, cols), F32),
             pltpu.VMEM((kh, 2 * cols), BF16),
             pltpu.VMEM((kh, 2 * cols), BF16),
+            pltpu.VMEM((cols, 512), F32),
             pltpu.VMEM((512, cols), F32),
             pltpu.VMEM((4, 2, 128, cols), F32),
             pltpu.VMEM((4, 2, 128, cols), F32),
@@ -298,7 +299,8 @@
             collective_id=0, has_side_effects=True, vmem_limit_bytes=56 * 1024 * 1024,
             dimension_semantics=("arbitrary",)),
         cost_estimate=pl.CostEstimate(flops=6 * 512 * depth * cols, bytes_accessed=4 * 512 * depth, transcendentals=0),
-    )(tau, vv_integrals, cycle_amps, ov_integrals)
+    )(tau.T, vv_integrals, cycle_amps, ov_integrals)
+    return both[0], both[1]
 
 
 def contract(left, right):

time: 89 us -> 67.7 us (0.76)
  local copies, waits for them, and re-layouts: 22.6 us -> 1.53 us
    unnamed x3 -> x0, local copies, waits for them, and re-layouts: 22.6 us -> none
    squeeze x0 -> x1, local copies, waits for them, and re-layouts: none -> 1.53 us  [fused(): return (both[0], both[1])]
where the time goes in v2:
time: 67.7 us; the launch traced here: 66.9 us
  Pallas kernels  64.8 us (96%)
  local copies, waits for them, and re-layouts  1.53 us (2%)
    pallas_call x1, Pallas kernels, fused(): pl.pallas_call(functools.partial(kernel, depth, tk, steps, kh), grid=(ste...  64.8 us
    squeeze x1, local copies, waits for them, and re-layouts, fused(): return (both[0], both[1])  1.53 us

profile of v2, /device:TPU:0, one launch (start us, length us, event | category | flops | bytes accessed | tf_op | source)
XLA Modules:
  0.0 66.9 jit_solution(3742540995643483186)
XLA Ops:
  0.6 64.8 %shard_map.59 = f32[2,128,128]{2,1,0:T(8,128)} custom-call(f32[10000,512]{1,0:T(8,128)} %bitcast.5, f32[10000,128]{1,0:T(8,128)} %vv_ref.1, f32[64,3000]{1,0:T(8,128)} %amps_ref.1, f32[3000,128]{1,0:T(8,128)} %ov_ref.1), custom_call_target="tpu_custom_call" | custom-call | flops 3932160000 | bytes 20480000 | tf_op jit(solution)/shard_map/pallas_call | solution.py:272
  65.4 1.5 %slice_bitcast_fusion = (f32[128,128]{1,0:T(8,128)}, f32[128,128]{1,0:T(8,128)}) fusion(f32[2,128,128]{2,1,0:T(8,128)} %shard_map.59), kind=kLoop, calls=%fused_computation | loop fusion | bytes 262144 | tf_op jit(solution)/shard_map/squeeze | solution.py:303

commit v3 on v0

v3 whole, which is shorter than its diff:
```python
import functools

import jax
import jax.numpy as jnp
from jax import lax
from jax.experimental import pallas as pl
from jax.experimental.pallas import tpu as pltpu
from jax.sharding import PartitionSpec as P

MESH = pl.DeviceIdType.MESH
F32 = jnp.float32
BF16 = jnp.bfloat16


def halves(x):
    hi = x.astype(BF16)
    lo = (x - hi.astype(F32)).astype(BF16)
    return hi, lo


def dot(a, b):
    return jnp.dot(a, b, preferred_element_type=F32)


def kernel(depth, tk, steps, kp, kq,
           tau_ref, vv_ref, amps_ref, ov_ref, out_ref,
           a_p, a_q, as_p, as_q, b_p, b_q, bs_p, bs_q, be_q, b_hi, b_lo, e_hi, e_lo,
           acc_t, acc, part, part_e, rs_c, rs_e, rs_l, fin_s, fin_r,
           sp_e, sp_x, sq_e, sq_x, rp, rq, y_send, yb_recv, be_send, be_recv,
           c_send, c_recv, e_send, e_recv, l_send, l_recv, f_send, f_recv):
    s = pl.program_id(0)
    w, n = lax.axis_index("wide"), lax.axis_index("narrow")
    z = w // 2
    y = w - 2 * z
    yp = 2 * z + 1 - y
    zn = z + 1 - 2 * (z % 2)
    zx = 3 - z
    zxn = 3 - zn
    end = (z == 0) | (z == 3)
    mid = (z == 1) | (z == 2)
    wn = w + 2 * (zn - z)
    wx = w + 2 * (zx - z)
    cols = ov_ref.shape[1]
    rows = amps_ref.shape[0]
    own = amps_ref.shape[1]
    kh = kp + kq
    left = own - kh - kp

    def remote(src, dst, send, recv, wt, nt):
        return pltpu.make_async_remote_copy(
            src_ref=src, dst_ref=dst, send_sem=send, recv_sem=recv, device_id=(wt, nt), device_id_type=MESH)

    def pe(zs, j):
        return remote(a_p.at[zs, j], a_p.at[zs, j], sp_e.at[zs, j], rp.at[zs, j], wn, n)

    def px(zs, j):
        return remote(a_p.at[zs, j], a_p.at[zs, j], sp_x.at[zs, j], rp.at[zs, j], wx, n)

    def qe(zs, j):
        return remote(a_q.at[zs, j], a_q.at[zs, j], sq_e.at[zs, j], rq.at[zs, j], wn, n)

    def qx(zs, j):
        return remote(a_q.at[zs, j], a_q.at[zs, j], sq_x.at[zs, j], rq.at[zs, j], wx, n)

    def ya_p():
        return remote(as_p, a_p.at[z, 1], y_send.at[0], rp.at[z, 1], yp, n)

    def ya_q():
        return remote(as_q, a_q.at[z, 1], y_send.at[1], rq.at[z, 1], yp, n)

    def yb_p():
        return remote(bs_p, b_p.at[1], y_send.at[2], yb_recv.at[0], yp, n)

    def yb_q():
        return remote(bs_q, b_q.at[1], y_send.at[3], yb_recv.at[1], yp, n)

    def be(j):
        return remote(b_q.at[j], be_q.at[j], be_send.at[j], be_recv.at[j], wn, n)

    def c_copy(zs, j, slot):
        return remote(part.at[zs, j], rs_c.at[slot, j], c_send.at[zs, j], c_recv.at[slot, j],
                      w if j == 0 else yp, zs)

    def e_copy(zs, j, slot):
        return remote(part_e.at[zs, j], rs_e.at[slot, j], e_send.at[zs, j], e_recv.at[slot, j],
                      w if j == 0 else yp, zs)

    def l_copy(zs, slot):
        return remote(acc.at[pl.ds(zs * 128, 128)], rs_l.at[slot], l_send.at[zs], l_recv.at[slot], w, zs)

    def f_copy():
        return remote(fin_s, fin_r, f_send, f_recv, wn, n)

    @pl.when(s == 0)
    def _():
        barrier = pltpu.get_barrier_semaphore()
        for k in range(4):
            @pl.when(n != k)
            def _():
                pl.semaphore_signal(barrier, inc=1, device_id=(w, k), device_id_type=MESH)
            pl.semaphore_signal(barrier, inc=1, device_id=(yp, k), device_id_type=MESH)
        pl.semaphore_signal(barrier, inc=1, device_id=(wn, n), device_id_type=MESH)

        @pl.when(mid)
        def _():
            pl.semaphore_signal(barrier, inc=1, device_id=(wx, n), device_id_type=MESH)

        zero = jnp.zeros((rows, 128), F32)

        @pl.when(y == 0)
        def _():
            a_p[z, 0] = amps_ref[:, :kp]
            a_q[z, 0] = amps_ref[:, kp:kh]
            as_p[...] = amps_ref[:, kh:kh + kp]
            as_q[:, kq - 128:] = zero
            as_q[:, :left] = amps_ref[:, kh + kp:own]

        @pl.when(y == 1)
        def _():
            as_p[...] = amps_ref[:, :kp]
            as_q[...] = amps_ref[:, kp:kh]
            a_p[z, 0] = amps_ref[:, kh:kh + kp]
            a_q[z, 0, :, kq - 128:] = zero
            a_q[z, 0, :, :left] = amps_ref[:, kh + kp:own]

        @pl.when(end)
        def _():
            pl.semaphore_wait(barrier, 8)

        @pl.when(mid)
        def _():
            pl.semaphore_wait(barrier, 9)

        ya_p().start()
        ya_q().start()
        pe(z, 0).start()

        @pl.when(end)
        def _():
            qe(z, 0).start()

        @pl.when(mid)
        def _():
            px(z, 0).start()
            qx(z, 0).start()

        pad = jnp.zeros((kq - left, cols), F32)

        @pl.when(y == 0)
        def _():
            b_p[0] = ov_ref[:kp]
            b_q[0] = ov_ref[kp:kh]
            bs_p[...] = ov_ref[kh:kh + kp]
            bs_q[:left] = ov_ref[kh + kp:own]
            bs_q[left:] = pad

        @pl.when(y == 1)
        def _():
            bs_p[...] = ov_ref[:kp]
            bs_q[...] = ov_ref[kp:kh]
            b_p[0] = ov_ref[kh:kh + kp]
            b_q[0, :left] = ov_ref[kh + kp:own]
            b_q[0, left:] = pad

        acc_t[...] = jnp.zeros(acc_t.shape, F32)

    @pl.when((s == 3) & mid)
    def _():
        pe(zn, 0).wait_recv()
        px(zn, 0).start()

    @pl.when(s == 4)
    def _():
        ya_p().wait_recv()
        pe(z, 1).start()

        @pl.when(mid)
        def _():
            px(z, 1).start()

    @pl.when(s == 5)
    def _():
        ya_q().wait_recv()

        @pl.when(end)
        def _():
            qe(z, 1).start()
            be(0).start()

        yb_q().start()
        yb_p().start()

        @pl.when(mid)
        def _():
            qe(zn, 0).wait_recv()
            qx(zn, 0).start()
            px(zx, 0).wait_recv()
            pe(zx, 0).start()

    def ladder(a, b):
        ah, al = halves(a)
        bh, bl = halves(b.T)
        both = dot(jnp.concatenate([bh, bl], axis=0), ah)
        acc_t[...] += both[:cols] + both[cols:] + dot(bh, al)

    @pl.when(s < steps - 1)
    def _():
        ladder(tau_ref[...], vv_ref[...])

    def split_b(ref, hi_ref, lo_ref, at, size):
        for j in range(2):
            hi, lo = halves(ref[j])
            hi_ref[at:at + size, j * cols:(j + 1) * cols] = hi
            lo_ref[at:at + size, j * cols:(j + 1) * cols] = lo

    def three(a, hi, lo):
        ah, al = halves(a.reshape(2 * rows, a.shape[-1]))
        return dot(ah, hi) + dot(ah, lo) + dot(al, hi)

    def place(r, ref, zs, copy):
        mine = pl.ds(pl.multiple_of(y * rows, rows), rows)
        other = pl.ds(pl.multiple_of((1 - y) * rows, rows), rows)
        for j in range(2):
            ref[zs, j, mine, :] = r[:rows, j * cols:(j + 1) * cols]
            ref[zs, j, other, :] = r[rows:, j * cols:(j + 1) * cols]

        @pl.when(zs != n)
        def _():
            copy(zs, 0, n).start()
        copy(zs, 1, n).start()

    def end_block(zs):
        place(three(a_p[zs], b_hi[:kp], b_lo[:kp]), part, zs, c_copy)

    def mid_block(zs):
        r = three(a_p[zs], b_hi[:kp], b_lo[:kp]) + three(a_q[zs], b_hi[kp:], b_lo[kp:])
        place(r, part, zs, c_copy)

    def far_block(zs):
        place(three(a_q[zs], e_hi[...], e_lo[...]), part_e, zs, e_copy)

    def gathered(ref, slots, copy):
        total = ref[n, 0]
        for k in range(4):
            @pl.when(n != k)
            def _():
                copy(k, 0, k).wait_recv()
                copy(k, 0, n).wait_send()

            @pl.when(n == k)
            def _():
                slots[k, 0] = jnp.zeros((128, cols), F32)
            copy(k, 1, k).wait_recv()
            copy(k, 1, n).wait_send()
            total += slots[k, 0] + slots[k, 1]
        return total

    def ladder_out():
        total = acc[pl.ds(pl.multiple_of(n * 128, 128), 128), :]
        for k in range(4):
            @pl.when(n != k)
            def _():
                l_copy(k, k).wait_recv()
                l_copy(k, n).wait_send()

            @pl.when(n == k)
            def _():
                rs_l[k] = jnp.zeros((128, cols), F32)
            total += rs_l[k]
        out_ref[0] = total

    @pl.when(s == steps - 1)
    def _():
        last = depth - (steps - 1) * tk
        a = tau_ref[...]
        a = jnp.where(lax.broadcasted_iota(jnp.int32, a.shape, 0) < last, a, 0.0)
        b = vv_ref[...]
        b = jnp.where(lax.broadcasted_iota(jnp.int32, b.shape, 0) < last, b, 0.0)
        ladder(a, b)

        @pl.when(mid)
        def _():
            pe(zn, 1).wait_recv()
            px(zn, 1).start()
            qx(z, 1).start()
            px(zxn, 0).wait_recv()
            pe(zxn, 0).start()
            px(zx, 1).wait_recv()
            pe(zx, 1).start()
            qe(zn, 1).wait_recv()
            qx(zn, 1).start()

        acc[...] = acc_t[...].T
        for k in range(4):
            @pl.when(n != k)
            def _():
                l_copy(k, n).start()

        yb_q().wait_recv()

        @pl.when(end)
        def _():
            be(1).start()

        split_b(b_q, b_hi, b_lo, kp, kq)
        yb_p().wait_recv()
        split_b(b_p, b_hi, b_lo, 0, kp)

        @pl.when(end)
        def _():
            end_block(z)
            for j in range(2):
                pe(zn, j).wait_recv()
            end_block(zn)
            for j in range(2):
                pe(zx, j).wait_recv()
            ladder_out()
            for j in range(2):
                pe(zxn, j).wait_recv()
            end_block(zxn)
            end_block(zx)
            total = gathered(part, rs_c, c_copy)
            f_copy().wait_recv()
            out_ref[1] = total + fin_r[...]
            for j in range(2):
                pe(z, j).wait_send()
                qe(z, j).wait_send()
                be(j).wait_send()

        @pl.when(mid)
        def _():
            px(zxn, 1).wait_recv()
            pe(zxn, 1).start()
            mid_block(z)
            mid_block(zn)
            for j in range(2):
                qx(zx, j).wait_recv()
            mid_block(zx)
            ladder_out()
            for j in range(2):
                be(j).wait_recv()
            split_b(be_q, e_hi, e_lo, 0, kq)
            far_block(z)
            far_block(zn)
            far_block(zx)
            for j in range(2):
                qx(zxn, j).wait_recv()
            far_block(zxn)
            mid_block(zxn)
            fin_s[...] = gathered(part_e, rs_e, e_copy)
            f_copy().start()
            out_ref[1] = gathered(part, rs_c, c_copy)
            for j in range(2):
                for k in (z, zx, zxn):
                    pe(k, j).wait_send()
                for k in (z, zn):
                    px(k, j).wait_send()
                    qx(k, j).wait_send()
            f_copy().wait_send()

        ya_p().wait_send()
        ya_q().wait_send()
        yb_p().wait_send()
        yb_q().wait_send()


def fused(tau, vv_integrals, cycle_amps, ov_integrals):
    depth = tau.shape[1]
    cols = vv_integrals.shape[1]
    rows, own = cycle_amps.shape
    tiles = -(-own // 256)
    kp = (tiles * 7 // 12) * 128
    kq = tiles * 128 - kp
    kh = kp + kq
    tk = 1280
    steps = -(-depth // tk)
    sem = pltpu.SemaphoreType.DMA
    both = pl.pallas_call(
        functools.partial(kernel, depth, tk, steps, kp, kq),
        grid=(steps,),
        out_shape=jax.ShapeDtypeStruct((2, 128, cols), F32),
        in_specs=[
            pl.BlockSpec((tk, tau.shape[0]), lambda s: (s, 0)),
            pl.BlockSpec((tk, cols), lambda s: (s, 0)),
            pl.BlockSpec((rows, own), lambda s: (0, 0)),
            pl.BlockSpec((own, cols), lambda s: (0, 0)),
        ],
        out_specs=pl.BlockSpec((2, 128, cols), lambda s: (0, 0, 0)),
        scratch_shapes=[
            pltpu.VMEM((4, 2, rows, kp), F32),
            pltpu.VMEM((4, 2, rows, kq), F32),
            pltpu.VMEM((rows, kp), F32),
            pltpu.VMEM((rows, kq), F32),
            pltpu.VMEM((2, kp, cols), F32),
            pltpu.VMEM((2, kq, cols), F32),
            pltpu.VMEM((kp, cols), F32),
            pltpu.VMEM((kq, cols), F32),
            pltpu.VMEM((2, kq, cols), F32),
            pltpu.VMEM((kh, 2 * cols), BF16),
            pltpu.VMEM((kh, 2 * cols), BF16),
            pltpu.VMEM((kq, 2 * cols), BF16),
            pltpu.VMEM((kq, 2 * cols), BF16),
            pltpu.VMEM((cols, 512), F32),
            pltpu.VMEM((512, cols), F32),
            pltpu.VMEM((4, 2, 128, cols), F32),
            pltpu.VMEM((4, 2, 128, cols), F32),
            pltpu.VMEM((4, 2, 128, cols), F32),
            pltpu.VMEM((4, 2, 128, cols), F32),
            pltpu.VMEM((4, 128, cols), F32),
            pltpu.VMEM((128, cols), F32),
            pltpu.VMEM((128, cols), F32),
            sem((4, 2)), sem((4, 2)), sem((4, 2)), sem((4, 2)), sem((4, 2)), sem((4, 2)),
            sem((4,)), sem((2,)), sem((2,)), sem((2,)),
            sem((4, 2)), sem((4, 2)), sem((4, 2)), sem((4, 2)), sem((4,)), sem((4,)), sem, sem,
        ],
        compiler_params=pltpu.CompilerParams(
            collective_id=0, has_side_effects=True, vmem_limit_bytes=56 * 1024 * 1024,
            dimension_semantics=("arbitrary",)),
        cost_estimate=pl.CostEstimate(flops=6 * 512 * depth * cols, bytes_accessed=4 * 512 * depth, transcendentals=0),
    )(tau.T, vv_integrals, cycle_amps, ov_integrals)
    return both[0], both[1]


def contract(left, right):
    return jnp.dot(left, right, precision=lax.Precision.HIGHEST, preferred_element_type=F32)


def plain(tau, vv_integrals, cycle_amps, ov_integrals):
    ladder_terms = contract(tau, vv_integrals)
    ladder_residual = lax.psum_scatter(ladder_terms, "narrow", scatter_dimension=0, tiled=True)
    cycle_terms = contract(lax.all_gather(cycle_amps, "wide", axis=0, tiled=True), ov_integrals)
    cycle_residual = lax.psum_scatter(cycle_terms, "narrow", scatter_dimension=0, tiled=True)
    return (ladder_residual, cycle_residual)


def solution(mesh):
    in_specs = (P(None, "narrow"), P("narrow", "wide"), P("wide", "narrow"), P("narrow", "wide"))
    out_specs = (P("narrow", "wide"), P("narrow", "wide"))
    small = mesh.shape["wide"] == 8 and mesh.shape["narrow"] == 4
    return jax.shard_map(fused if small else plain, mesh=mesh, in_specs=in_specs, out_specs=out_specs, check_vma=False)
```

time: 147 us -> 58 us (0.39)
  waiting for transfers between devices: 86.4 us -> 0 us
  Pallas kernels: 0 us -> 55.6 us
  matrix products: 44.6 us -> 0 us
  between operations: 15.5 us -> 0.64 us
  local copies, waits for them, and re-layouts: 0.01 us -> 1.53 us
    all_gather x1 -> x0, waiting for transfers between devices: 67.4 us -> none  [cycle_terms_of(): lax.all_gather(cycle_amps, 'wide', axis=0, tiled=True)]
    pallas_call x0 -> x1, Pallas kernels: none -> 55.6 us  [fused(): pl.pallas_call(functools.partial(kernel, depth, tk, steps, kp, kq), grid=...]
    dot_general x2 -> x0, matrix products: 44.6 us -> none  [contract(): jnp.dot(left, right, precision=lax.Precision.HIGHEST, preferred_element_t...]
    reduce_scatter x2 -> x0, waiting for transfers between devices: 18.2 us -> none  [the longest x1 18.2 us: body(): lax.psum_scatter(cycle_terms, 'narrow', scatter_dimension=0, tiled=True)]
    squeeze x0 -> x1, local copies, waits for them, and re-layouts: none -> 1.53 us  [fused(): return (both[0], both[1])]
  transfers between devices with their start and end apart: 3 -> 0, of which waited for: 2 -> 0; matrix products, arithmetic and copies ran while one was open for 30% -> 0% of each run, Pallas kernels for 0% -> 0%
where the time goes in v3:
time: 58 us; the launch traced here: 57.8 us
  Pallas kernels  55.6 us (96%)
  local copies, waits for them, and re-layouts  1.53 us (3%)
  between operations  0.64 us (1%)
    pallas_call x1, Pallas kernels, fused(): pl.pallas_call(functools.partial(kernel, depth, tk, steps, kp, kq), grid=...  55.6 us
    squeeze x1, local copies, waits for them, and re-layouts, fused(): return (both[0], both[1])  1.53 us

profile of v3, /device:TPU:0, one launch (start us, length us, event | category | flops | bytes accessed | tf_op | source)
XLA Modules:
  0.0 57.8 jit_solution(3051874302816404031)
XLA Ops:
  0.6 55.6 %shard_map.59 = f32[2,128,128]{2,1,0:T(8,128)} custom-call(f32[10000,512]{1,0:T(8,128)} %bitcast.5, f32[10000,128]{1,0:T(8,128)} %vv_ref.1, f32[64,3000]{1,0:T(8,128)} %amps_ref.1, f32[3000,128]{1,0:T(8,128)} %ov_ref.1), custom_call_target="tpu_custom_call" | custom-call | flops 3932160000 | bytes 20480000 | tf_op jit(solution)/shard_map/pallas_call | solution.py:378
  56.3 1.5 %slice_bitcast_fusion = (f32[128,128]{1,0:T(8,128)}, f32[128,128]{1,0:T(8,128)}) fusion(f32[2,128,128]{2,1,0:T(8,128)} %shard_map.59), kind=kLoop, calls=%fused_computation | loop fusion | bytes 262144 | tf_op jit(solution)/shard_map/squeeze | solution.py:421

commit v4 on v3

--- a/solution.py
+++ b/solution.py
@@ -164,12 +164,12 @@
 
         acc_t[...] = jnp.zeros(acc_t.shape, F32)
 
-    @pl.when((s == 3) & mid)
+    @pl.when((s == 1) & mid)
     def _():
         pe(zn, 0).wait_recv()
         px(zn, 0).start()
 
-    @pl.when(s == 4)
+    @pl.when(s == 2)
     def _():
         ya_p().wait_recv()
         pe(z, 1).start()
@@ -177,25 +177,43 @@
         @pl.when(mid)
         def _():
             px(z, 1).start()
-
-    @pl.when(s == 5)
-    def _():
+            px(zx, 0).wait_recv()
+            pe(zx, 0).start()
+
         ya_q().wait_recv()
+        yb_q().start()
+        yb_p().start()
 
         @pl.when(end)
         def _():
             qe(z, 1).start()
             be(0).start()
 
-        yb_q().start()
-        yb_p().start()
-
-        @pl.when(mid)
-        def _():
-            qe(zn, 0).wait_recv()
-            qx(zn, 0).start()
-            px(zx, 0).wait_recv()
-            pe(zx, 0).start()
+        @pl.when(mid)
+        def _():
+            qx(z, 1).start()
+
+    @pl.when((s == 3) & mid)
+    def _():
+        qe(zn, 0).wait_recv()
+        qx(zn, 0).start()
+
+    @pl.when((s == 4) & mid)
+    def _():
+        pe(zn, 1).wait_recv()
+        px(zn, 1).start()
+        px(zxn, 0).wait_recv()
+        pe(zxn, 0).start()
+
+    @pl.when((s == 5) & mid)
+    def _():
+        px(zx, 1).wait_recv()
+        pe(zx, 1).start()
+
+    @pl.when((s == 6) & mid)
+    def _():
+        qe(zn, 1).wait_recv()
+        qx(zn, 1).start()
 
     def ladder(a, b):
         ah, al = halves(a)
@@ -277,18 +295,6 @@
         b = vv_ref[...]
         b = jnp.where(lax.broadcasted_iota(jnp.int32, b.shape, 0) < last, b, 0.0)
         ladder(a, b)
-
-        @pl.when(mid)
-        def _():
-            pe(zn, 1).wait_recv()
-            px(zn, 1).start()
-            qx(z, 1).start()
-            px(zxn, 0).wait_recv()
-            pe(zxn, 0).start()
-            px(zx, 1).wait_recv()
-            pe(zx, 1).start()
-            qe(zn, 1).wait_recv()
-            qx(zn, 1).start()
 
         acc[...] = acc_t[...].T
         for k in range(4):

time: 58 us -> 60.1 us (1.036)
  Pallas kernels: 55.6 us -> 57.8 us
    pallas_call x1, Pallas kernels: 55.6 us -> 57.8 us  [fused(): pl.pallas_call(functools.partial(kernel, depth, tk, steps, kp, kq), grid=...]
where the time goes in v4:
time: 60.1 us; the launch traced here: 59.9 us
  Pallas kernels  57.8 us (96%)
  local copies, waits for them, and re-layouts  1.53 us (3%)
  between operations  0.64 us (1%)
    pallas_call x1, Pallas kernels, fused(): pl.pallas_call(functools.partial(kernel, depth, tk, steps, kp, kq), grid=...  57.8 us
    squeeze x1, local copies, waits for them, and re-layouts, fused(): return (both[0], both[1])  1.53 us

profile of v4, /device:TPU:0, one launch (start us, length us, event | category | flops | bytes accessed | tf_op | source)
XLA Modules:
  0.0 59.9 jit_solution(7068727481270566615)
XLA Ops:
  0.6 57.8 %shard_map.59 = f32[2,128,128]{2,1,0:T(8,128)} custom-call(f32[10000,512]{1,0:T(8,128)} %bitcast.5, f32[10000,128]{1,0:T(8,128)} %vv_ref.1, f32[64,3000]{1,0:T(8,128)} %amps_ref.1, f32[3000,128]{1,0:T(8,128)} %ov_ref.1), custom_call_target="tpu_custom_call" | custom-call | flops 3932160000 | bytes 20480000 | tf_op jit(solution)/shard_map/pallas_call | solution.py:384
  58.4 1.5 %slice_bitcast_fusion = (f32[128,128]{1,0:T(8,128)}, f32[128,128]{1,0:T(8,128)}) fusion(f32[2,128,128]{2,1,0:T(8,128)} %shard_map.59), kind=kLoop, calls=%fused_computation | loop fusion | bytes 262144 | tf_op jit(solution)/shard_map/squeeze | solution.py:427

commit v5 on v3

--- a/solution.py
+++ b/solution.py
@@ -197,6 +197,21 @@
             px(zx, 0).wait_recv()
             pe(zx, 0).start()
 
+    @pl.when((s == 6) & mid)
+    def _():
+        pe(zn, 1).wait_recv()
+        px(zn, 1).start()
+        qx(z, 1).start()
+        px(zxn, 0).wait_recv()
+        pe(zxn, 0).start()
+
+    @pl.when((s == 7) & mid)
+    def _():
+        px(zx, 1).wait_recv()
+        pe(zx, 1).start()
+        qe(zn, 1).wait_recv()
+        qx(zn, 1).start()
+
     def ladder(a, b):
         ah, al = halves(a)
         bh, bl = halves(b.T)
@@ -277,18 +292,6 @@
         b = vv_ref[...]
         b = jnp.where(lax.broadcasted_iota(jnp.int32, b.shape, 0) < last, b, 0.0)
         ladder(a, b)
-
-        @pl.when(mid)
-        def _():
-            pe(zn, 1).wait_recv()
-            px(zn, 1).start()
-            qx(z, 1).start()
-            px(zxn, 0).wait_recv()
-            pe(zxn, 0).start()
-            px(zx, 1).wait_recv()
-            pe(zx, 1).start()
-            qe(zn, 1).wait_recv()
-            qx(zn, 1).start()
 
         acc[...] = acc_t[...].T
         for k in range(4):

time: 58 us -> 58 us (level)
  no operation moved by 1% of the time
where the time goes in v5:
time: 58 us; the launch traced here: 57.8 us
  Pallas kernels  55.6 us (96%)
  local copies, waits for them, and re-layouts  1.53 us (3%)
  between operations  0.64 us (1%)
    pallas_call x1, Pallas kernels, fused(): pl.pallas_call(functools.partial(kernel, depth, tk, steps, kp, kq), grid=...  55.6 us
    squeeze x1, local copies, waits for them, and re-layouts, fused(): return (both[0], both[1])  1.53 us

profile of v5, /device:TPU:0, one launch (start us, length us, event | category | flops | bytes accessed | tf_op | source)
XLA Modules:
  0.0 57.8 jit_solution(12910550115540115614)
XLA Ops:
  0.6 55.6 %shard_map.59 = f32[2,128,128]{2,1,0:T(8,128)} custom-call(f32[10000,512]{1,0:T(8,128)} %bitcast.5, f32[10000,128]{1,0:T(8,128)} %vv_ref.1, f32[64,3000]{1,0:T(8,128)} %amps_ref.1, f32[3000,128]{1,0:T(8,128)} %ov_ref.1), custom_call_target="tpu_custom_call" | custom-call | flops 3932160000 | bytes 20480000 | tf_op jit(solution)/shard_map/pallas_call | solution.py:381
  56.3 1.5 %slice_bitcast_fusion = (f32[128,128]{1,0:T(8,128)}, f32[128,128]{1,0:T(8,128)}) fusion(f32[2,128,128]{2,1,0:T(8,128)} %shard_map.59), kind=kLoop, calls=%fused_computation | loop fusion | bytes 262144 | tf_op jit(solution)/shard_map/squeeze | solution.py:424
